TPU v7x, 512 devices: a whole 4x8x8 slice. The times are simulated.
512 devices in a mesh: segment: 16 (over y, core), tile: 32 (over z, x).
Axes of the slice: x: 4, y: 8, z: 8, core: 2. Of those that a mesh axis runs over, the one named last changes fastest.
Arguments:
- tile_mask_amplitude: bfloat16 [512, 256, 256], P('tile', 'segment'), may hold values from -4 to 4
- tile_target_images: bfloat16 [512, 256, 256], P('tile', 'segment'), may hold values from 0 to 1
- spectra: float32 [12, 2, 31, 31], replicated, may hold values from -6 to 6
- slot_dose_scale: float32 [512], P('tile'), may hold values from 0.5 to 2
- slot_row: int32 [512], P('tile'), may hold values from -1 to 31, as said below
- side_source: int32 [512, 2], P('tile'), may hold values from -1 to 11, as said below
Outputs:
- corrected_mask: bfloat16 [512, 256, 256], P('tile', 'segment')
- resist_image: float32 [512, 256, 256], P('tile', 'segment')
Inputs may be any that keep to these rules, and one draw needn't show every extreme that they name: `slot_row`: in each tile owner's 16 slots the patterned tiles come first, with strictly rising tile rows below 32, and -1 marks the empty slots after them; every owner has at least 4 patterned tiles and at most 12, and some owner has exactly 12; every owner holds tile row 31. `side_source`: an entry names the slot of the neighbouring tile owner that holds the same tile row as this slot; it is -1 for empty slots, at the window's ends and where that tile is not patterned.
All inputs are finite; a program needn't handle non-finite values.
Results may differ from a plain program's by a relative error of at most 0.0075.
Values may be sent and summed in bfloat16 or wider, within the bound.
No kernel may reach another device: no remote copies, remote signals or barrier semaphores. Data moves between devices by JAX's collectives and lax.ppermute only.
A program may use at most 64 MiB of HBM per device.

v0:
```python
import math
import jax
import jax.numpy as jnp
from jax import lax
from jax.sharding import PartitionSpec as P

RB = 8
ITERS = 2
STEEPNESS = 1.5
THRESHOLD = 2.0
STEP_GAIN = 0.5


def passed_along(block, axis, distance):
    devices = range(lax.axis_size(axis))
    route = [(i - distance, i) for i in devices if i - distance in devices]
    return lax.ppermute(block, axis, route)


def with_halo(cells, sides, width):
    for axis, dim in sides:
        count = lax.axis_size(axis)
        head = lax.slice_in_dim(cells, 0, width, axis=dim)
        tail = lax.slice_in_dim(cells, cells.shape[dim] - width, cells.shape[dim], axis=dim)
        cells = jnp.concatenate(
            [
                lax.ppermute(tail, axis, [(i, (i + 1) % count) for i in range(count)]),
                cells,
                lax.ppermute(head, axis, [((i + 1) % count, i) for i in range(count)]),
            ],
            axis=dim,
        )
    return cells


def wave_tables(length, freq_count):
    position = jnp.arange(length, dtype=jnp.int32)
    frequency = jnp.arange(freq_count, dtype=jnp.int32) - freq_count // 2
    phase_index = position[:, None] * frequency[None, :] % length
    angle_rad = phase_index.astype(jnp.float32) * jnp.float32(2.0 * math.pi / length)
    return (jnp.cos(angle_rad), jnp.sin(angle_rad))


def transform_tables(length, freq_count):
    cosine, sine_part = wave_tables(length, freq_count)
    norm_scale = jnp.float32(1.0 / math.sqrt(length))
    forward_cols = jnp.concatenate([cosine * norm_scale, -(sine_part * norm_scale)], 1).astype(
        jnp.bfloat16
    )
    forward_rows = jnp.concatenate([cosine * norm_scale, sine_part * norm_scale], 1).astype(
        jnp.bfloat16
    )
    inverse_rows = jnp.concatenate([cosine, sine_part], 1).astype(jnp.bfloat16)
    cosine_low = cosine.T.astype(jnp.bfloat16)
    sine_low = sine_part.T.astype(jnp.bfloat16)
    inverse_cols = jnp.concatenate(
        [jnp.concatenate([cosine_low, sine_low], 1), jnp.concatenate([-sine_low, cosine_low], 1)], 0
    )
    return (forward_cols, forward_rows, inverse_rows, inverse_cols)


def blur_weights(radius):
    offsets = jnp.arange(2 * radius + 1, dtype=jnp.float32) - radius
    spread_width = radius / 2.0
    weights = jnp.exp(-offsets * offsets / (2.0 * spread_width * spread_width))
    return weights / jnp.sum(weights)


def spectrum_part(tile_rows, rows_table, forward_cols, freq_count):
    y_part = jnp.einsum(
        "nry,yb->nrb", tile_rows, forward_cols, preferred_element_type=jnp.float32
    ).astype(jnp.bfloat16)
    inner = jnp.einsum("ra,nrb->nab", rows_table, y_part, preferred_element_type=jnp.float32)
    real_part = inner[:, :freq_count, :freq_count] + inner[:, freq_count:, freq_count:]
    imag_part = inner[:, :freq_count, freq_count:] - inner[:, freq_count:, :freq_count]
    return jnp.stack([real_part, imag_part], 1)


def intensity_rows(spectrum, spectra, rows_inverse, inverse_cols, tile_edge):
    item_count = spectrum.shape[0]
    row_count = rows_inverse.shape[0]
    freq_count = spectra.shape[2]
    kernel_count = spectra.shape[0]
    block_len = 8
    spec_real = spectra[:, 0]
    spec_imag = spectra[:, 1]

    def one_block(spec_block):
        mask_real = spec_block[:, None, 0]
        mask_imag = spec_block[:, None, 1]
        prod_real = (spec_real * mask_real - spec_imag * mask_imag).astype(jnp.bfloat16)
        prod_imag = (spec_real * mask_imag + spec_imag * mask_real).astype(jnp.bfloat16)
        right_block = jnp.concatenate(
            [
                jnp.concatenate([prod_real, prod_imag], 3),
                jnp.concatenate([-prod_imag, prod_real], 3),
            ],
            2,
        )
        field_a = jnp.einsum(
            "ra,nkab->nkrb", rows_inverse, right_block, preferred_element_type=jnp.float32
        )
        field_a = (field_a * jnp.float32(1.0 / freq_count)).astype(jnp.bfloat16)
        field_full = jnp.einsum(
            "nkrb,by->nkry", field_a, inverse_cols, preferred_element_type=jnp.float32
        )
        squares = jnp.sum(field_full * field_full, axis=1)
        return (squares[..., :tile_edge] + squares[..., tile_edge:]) * jnp.float32(
            1.0 / kernel_count
        )

    grouped = spectrum.reshape(item_count // block_len, block_len, 2, freq_count, freq_count)
    return lax.map(one_block, grouped).reshape(item_count, row_count, tile_edge)


def pick_bands(received, source):
    valid = (source >= 0).astype(jnp.float32)
    taken = jnp.take(received, jnp.maximum(source, 0), axis=0)
    return taken * valid[:, None, None]


def body(tile_mask_amplitude, tile_target_images, spectra, slot_dose_scale, slot_row, side_source):
    slot_count, row_count, tile_edge = tile_mask_amplitude.shape
    freq_count = spectra.shape[2]
    segment_index = lax.axis_index("segment")
    last_segment = lax.axis_size("segment") - 1
    forward_cols, forward_rows, inverse_rows, inverse_cols = transform_tables(tile_edge, freq_count)
    rows_inverse = lax.dynamic_slice_in_dim(inverse_rows, segment_index * row_count, row_count, 0)
    weights = blur_weights(RB)
    weight = slot_dose_scale * (slot_row >= 0).astype(jnp.float32)
    slot_index = jnp.arange(slot_count, dtype=jnp.int32)
    prev_row = jnp.concatenate([jnp.full((1,), -7, jnp.int32), slot_row[:-1]])
    up_ok = (slot_index > 0) & (prev_row >= 0) & (slot_row >= 0) & (prev_row == slot_row - 1)
    down_ok = jnp.concatenate([up_ok[1:], jnp.zeros((1,), dtype=bool)])
    up_weight = up_ok.astype(jnp.float32)[:, None, None]
    down_weight = down_ok.astype(jnp.float32)[:, None, None]
    zero_rim = jnp.zeros((1, RB, tile_edge), jnp.float32)
    mask_now = tile_mask_amplitude
    resist = jnp.zeros((slot_count, row_count, tile_edge), jnp.float32)
    for sweep in range(ITERS):
        work_tiles = mask_now
        whole_tiles = lax.all_gather(work_tiles, "segment", axis=1, tiled=True)
        spectrum = spectrum_part(whole_tiles, forward_rows, forward_cols, freq_count)
        intensity = intensity_rows(spectrum, spectra, rows_inverse, inverse_cols, tile_edge)
        intensity = intensity * weight[:, None, None]
        from_left = passed_along(intensity[:, :, tile_edge - RB :], "tile", 1)
        from_right = passed_along(intensity[:, :, :RB], "tile", -1)
        left_band = pick_bands(from_left, side_source[:, 0])
        right_band = pick_bands(from_right, side_source[:, 1])
        padded = jnp.concatenate([left_band, intensity, right_band], 2)
        horiz_blur = weights[0] * padded[:, :, 0:tile_edge]
        for shift_by in range(1, 2 * RB + 1):
            horiz_blur = (
                horiz_blur + weights[shift_by] * padded[:, :, shift_by : shift_by + tile_edge]
            )
        extended = with_halo(horiz_blur.astype(jnp.bfloat16), (("segment", 1),), RB).astype(
            horiz_blur.dtype
        )
        upper_rim = extended[:, :RB]
        lower_rim = extended[:, row_count + RB :]
        upper_next = jnp.concatenate([zero_rim, upper_rim[:-1]], 0) * up_weight
        lower_next = jnp.concatenate([lower_rim[1:], zero_rim], 0) * down_weight
        upper_rim = jnp.where(segment_index == 0, upper_next, upper_rim)
        lower_rim = jnp.where(segment_index == last_segment, lower_next, lower_rim)
        vert_padded = jnp.concatenate([upper_rim, horiz_blur, lower_rim], 1)
        vert_blur = weights[0] * vert_padded[:, 0:row_count, :]
        for shift_by in range(1, 2 * RB + 1):
            vert_blur = (
                vert_blur + weights[shift_by] * vert_padded[:, shift_by : shift_by + row_count, :]
            )
        resist = jax.nn.sigmoid(STEEPNESS * (vert_blur - THRESHOLD))
        mask_now = (
            mask_now.astype(jnp.float32)
            + STEP_GAIN * (tile_target_images.astype(jnp.float32) - resist)
        ).astype(jnp.bfloat16)
    return (mask_now, resist)


def solution(mesh):
    in_specs = (
        P("tile", "segment", None),
        P("tile", "segment", None),
        P(),
        P("tile"),
        P("tile"),
        P("tile", None),
    )
    out_specs = (P("tile", "segment", None), P("tile", "segment", None))
    return jax.shard_map(body, mesh=mesh, in_specs=in_specs, out_specs=out_specs, check_vma=False)
```

profile of v0, /device:TPU:199, one launch (start us, length us, event | category | flops | bytes accessed | tf_op | source)
XLA Modules:
  0.0 219.9 jit_solution(1284356911872364960)
XLA Ops:
  16.5 38.4 %all-gather.3.cloned.1.call-done = bf16[16,256,256]{2,1,0:T(8,128)(2,1)} async-done(((bf16[16,16,256]{2,1,0:T(8,128)(2,1)}), bf16[16,256,256]{2,1,0:T(8,128)(2,1)}) %all-gather.3.cloned.1.call-update) | async-done | bytes 2097168 | tf_op jit(solution)/shard_map/all_gather | solution.py:142
  55.0 2.5 %fusion.67 = f32[16,62,62]{1,2,0:T(8,128)S(1)} fusion(bf16[16,256,256]{2,1,0:T(8,128)(2,1)} %all-gather.3.cloned.1.call-done, bf16[256,31]{0,1:T(8,128)(2,1)S(1)} %get-tuple-element.236, bf16[256,31]{0,1:T(8,128)(2,1)S(1)} %get-tuple-element.234, bf16[256,31]{0,1:T(8,128)(2,1)S(1)} %get-tuple-element.235), kind=kOutput, calls=%fused_computation.64 | convolution fusion | flops 161894400 | bytes 2390784 | tf_op jit(solution)/shard_map/ra,nrb->nab/dot_general | solution.py:73
  58.9 8.2 %while.20 = (s32[]{:T(128)}, f32[2,8,16,256]{3,2,1,0:T(8,128)}, f32[12,1,31,31]{3,2,0,1:T(8,128)S(1)}, f32[2,8,2,31,31]{4,1,3,2,0:T(8,128)S(1)}, f32[12,1,31,31]...) while((s32[]{:T(128)}, f32[2,8,16,256]{3,2,1,0:T(8,128)}, ...), condition=%wide.region_3.4_spmd, body=%wide.region_1.3_spmd.sunk | while | flops 115241184 | bytes 2505049 | solution.py:113
  59.7 2.6 %multiply_reduce_fusion.4 = f32[8,16,512]{2,1,0:T(8,128)S(1)} fusion(bf16[8,12,31,31]{3,2,1,0:T(8,128)(2,1)S(1)} %get-tuple-element.326, bf16[8,12,31,31]{3,2,1,0:T(8,128)(2,1)S(1)} %fusion.337, bf16[8,12,31,31]{3,2,1,0:T(8,128)(2,1)S(1)} %get-tuple-element.327, bf16[62,512]{1,0:T(8,128)(2,1)} %get-tuple-element.361, ...), kind=kOutput, calls=%fused_computation.4.clone.1 | convolution fusion | flops 113976320 | bytes 881152 | tf_op jit(solution)/shard_map/while/body/eval_jaxpr/nkrb,by->nkry/dot_general | solution.py:104
  63.8 2.6 %multiply_reduce_fusion.4 = f32[8,16,512]{2,1,0:T(8,128)S(1)} fusion(bf16[8,12,31,31]{3,2,1,0:T(8,128)(2,1)S(1)} %get-tuple-element.326, bf16[8,12,31,31]{3,2,1,0:T(8,128)(2,1)S(1)} %fusion.337, bf16[8,12,31,31]{3,2,1,0:T(8,128)(2,1)S(1)} %get-tuple-element.327, bf16[62,512]{1,0:T(8,128)(2,1)} %get-tuple-element.361, ...), kind=kOutput, calls=%fused_computation.4.clone.1 | convolution fusion | flops 113976320 | bytes 881152 | tf_op jit(solution)/shard_map/while/body/eval_jaxpr/nkrb,by->nkry/dot_general | solution.py:104
  68.2 4.5 %collective-permute-start = (f32[16,16,8]{2,1,0:T(8,128)S(1)}, f32[16,16,8]{2,1,0:T(8,128)S(1)}, u32[]{:S(2)}, u32[]{:S(2)}) collective-permute-start(f32[16,16,8]{2,1,0:T(8,128)S(1)} %get-tuple-element.203), channel_id=1, source_target_pairs={{0,1},{1,2},{2,3},{3,4},{4,5},{5,6},{6,7},{7,8},{8,9},{9,10},{10,1... | collective-permute-start | bytes 24584 | tf_op jit(solution)/shard_map/ppermute | solution.py:17
  74.1 2.1 collective-permute-start.1
  77.9 5.9 %collective-permute-done.1 = f32[16,16,8]{2,1,0:T(8,128)S(1)} collective-permute-done((f32[16,16,8]{2,1,0:T(8,128)S(1)}, f32[16,16,8]{2,1,0:T(8,128)S(1)}, u32[]{:S(2)}, u32[]{:S(2)}) %collective-permute-start.1) | collective-permute-done | bytes 8224 | tf_op jit(solution)/shard_map/ppermute | solution.py:17
  84.5 12.2 %fusion.315 = (bf16[16,16,256]{2,1,0:T(8,128)(2,1)S(1)}, f32[16,16,256]{2,1,0:T(8,128)S(1)}) fusion(f32[16,16,8]{2,1,0:T(8,128)S(1)} %select_multiply_fusion.1, f32[16,16,256]{2,1,0:T(8,128)S(1)} %bitcast_multiply_fusion.1, f32[]{:T(128)} %bitcast.49, f32[]{:T(128)} %bitcast.48, f32[]{:T(128)} %bitcast.47, f32[]{:T(128)} %bitcast.46, f32[]{:T(128)} %bitcast.45, ...), kind=kLoop, calls=%fused_computation.474 | loop fusion | flops 3276800 | bytes 671812 | tf_op jit(solution)/shard_map/convert_element_type | solution.py:156
  96.7 2.2 collective-permute-start.2
  100.2 2.4 %collective-permute-done.3 = bf16[16,8,256]{2,1,0:T(8,128)(2,1)S(1)} collective-permute-done((bf16[16,8,256]{2,1,0:T(8,128)(2,1)S(1)}, bf16[16,8,256]{2,1,0:T(8,128)(2,1)S(1)}, u32[]{:S(2)}, u32[]{:S(2)}) %collective-permute-start.3) | collective-permute-done | bytes 65568 | tf_op jit(solution)/shard_map/ppermute | solution.py:29
  102.8 11.4 %fusion.76 = bf16[16,16,256]{2,1,0:T(8,128)(2,1)S(1)} fusion(bf16[16,16,256]{2,1,0:T(8,128)(2,1)S(1)} %copy-done.2, f32[16,16,256]{2,1,0:T(8,128)S(1)} %get-tuple-element.174, f32[16,8,256]{2,1,0:T(8,128)S(1)} %get-tuple-element.200, f32[16,8,256]{2,1,0:T(8,128)S(1)} %get-tuple-element.199, bf16[16,16,256]{2,1,0:T(8,128)(2,1)S(1)} %copy-done.4, ...), kind=kLoop, calls=%fused_computation.185 | loop fusion | flops 3932160 | bytes 917572 | tf_op jit(solution)/shard_map/convert_element_type | solution.py:175
  115.6 38.8 %all-gather.5.cloned.1.call-done = bf16[16,256,256]{2,0,1:T(8,128)(2,1)} async-done(((bf16[16,16,256]{2,0,1:T(8,128)(2,1)}), bf16[16,256,256]{2,0,1:T(8,128)(2,1)}) %all-gather.5.cloned.1.call-update) | async-done | bytes 2097168 | tf_op jit(solution)/shard_map/all_gather | solution.py:142
  154.4 2.5 %fusion.71 = f32[16,62,62]{1,2,0:T(8,128)S(1)} fusion(bf16[16,256,256]{2,0,1:T(8,128)(2,1)} %all-gather.5.cloned.1.call-done, bf16[256,31]{0,1:T(8,128)(2,1)S(1)} %get-tuple-element.236, bf16[256,31]{0,1:T(8,128)(2,1)S(1)} %get-tuple-element.234, bf16[256,31]{0,1:T(8,128)(2,1)S(1)} %copy-done.6), kind=kOutput, calls=%fused_computation.66 | convolution fusion | flops 161894400 | bytes 2390784 | tf_op jit(solution)/shard_map/ra,nrb->nab/dot_general | solution.py:73
  158.4 8.2 %while.21 = (s32[]{:T(128)}, f32[2,8,16,256]{3,2,1,0:T(8,128)}, f32[12,1,31,31]{3,2,0,1:T(8,128)S(1)}, f32[2,8,2,31,31]{4,1,3,2,0:T(8,128)S(1)}, f32[12,1,31,31]...) while((s32[]{:T(128)}, f32[2,8,16,256]{3,2,1,0:T(8,128)}, ...), condition=%wide.region_6.8_spmd, body=%wide.region_4.7_spmd.sunk | while | flops 115241184 | bytes 2505049 | solution.py:113
  159.2 2.6 %multiply_reduce_fusion.5 = f32[8,16,512]{2,1,0:T(8,128)S(1)} fusion(bf16[8,12,31,31]{3,2,1,0:T(8,128)(2,1)S(1)} %get-tuple-element.337, bf16[8,12,31,31]{3,2,1,0:T(8,128)(2,1)S(1)} %fusion.342, bf16[8,12,31,31]{3,2,1,0:T(8,128)(2,1)S(1)} %get-tuple-element.338, bf16[62,512]{1,0:T(8,128)(2,1)} %get-tuple-element.385, ...), kind=kOutput, calls=%fused_computation.31.clone.1 | convolution fusion | flops 113976320 | bytes 881152 | tf_op jit(solution)/shard_map/while/body/eval_jaxpr/nkrb,by->nkry/dot_general | solution.py:104
  163.3 2.6 %multiply_reduce_fusion.5 = f32[8,16,512]{2,1,0:T(8,128)S(1)} fusion(bf16[8,12,31,31]{3,2,1,0:T(8,128)(2,1)S(1)} %get-tuple-element.337, bf16[8,12,31,31]{3,2,1,0:T(8,128)(2,1)S(1)} %fusion.342, bf16[8,12,31,31]{3,2,1,0:T(8,128)(2,1)S(1)} %get-tuple-element.338, bf16[62,512]{1,0:T(8,128)(2,1)} %get-tuple-element.385, ...), kind=kOutput, calls=%fused_computation.31.clone.1 | convolution fusion | flops 113976320 | bytes 881152 | tf_op jit(solution)/shard_map/while/body/eval_jaxpr/nkrb,by->nkry/dot_general | solution.py:104
  167.8 4.5 %collective-permute-start.4 = (f32[16,16,8]{2,1,0:T(8,128)S(1)}, f32[16,16,8]{2,1,0:T(8,128)S(1)}, u32[]{:S(2)}, u32[]{:S(2)}) collective-permute-start(f32[16,16,8]{2,1,0:T(8,128)S(1)} %get-tuple-element.197), channel_id=1, source_target_pairs={{0,1},{1,2},{2,3},{3,4},{4,5},{5,6},{6,7},{7,8},{8,9},{9,10},{10,1... | collective-permute-start | bytes 24584 | tf_op jit(solution)/shard_map/ppermute | solution.py:17
  172.2 1.9 collective-permute-start.5
  175.9 6.1 %collective-permute-done.5 = f32[16,16,8]{2,1,0:T(8,128)S(1)} collective-permute-done((f32[16,16,8]{2,1,0:T(8,128)S(1)}, f32[16,16,8]{2,1,0:T(8,128)S(1)}, u32[]{:S(2)}, u32[]{:S(2)}) %collective-permute-start.5) | collective-permute-done | bytes 8224 | tf_op jit(solution)/shard_map/ppermute | solution.py:17
  182.7 12.2 %fusion.312 = (bf16[16,16,256]{2,1,0:T(8,128)(2,1)S(1)}, f32[16,16,256]{2,1,0:T(8,128)S(1)}) fusion(f32[16,16,8]{2,1,0:T(8,128)S(1)} %select_multiply_fusion, f32[16,16,256]{2,1,0:T(8,128)S(1)} %bitcast_multiply_fusion, f32[]{:T(128)} %bitcast.49, f32[]{:T(128)} %bitcast.48, f32[]{:T(128)} %bitcast.47, f32[]{:T(128)} %bitcast.46, f32[]{:T(128)} %bitcast.45, ...), kind=kLoop, calls=%fused_computation.472 | loop fusion | flops 3276800 | bytes 671812 | tf_op jit(solution)/shard_map/convert_element_type | solution.py:156
  194.9 2.1 collective-permute-start.6
  198.4 2.4 %collective-permute-done.7 = bf16[16,8,256]{2,1,0:T(8,128)(2,1)S(1)} collective-permute-done((bf16[16,8,256]{2,1,0:T(8,128)(2,1)S(1)}, bf16[16,8,256]{2,1,0:T(8,128)(2,1)S(1)}, u32[]{:S(2)}, u32[]{:S(2)}) %collective-permute-start.7) | collective-permute-done | bytes 65568 | tf_op jit(solution)/shard_map/ppermute | solution.py:29
  201.0 12.1 %fusion.79 = (bf16[16,16,256]{2,1,0:T(8,128)(2,1)}, f32[16,16,256]{2,1,0:T(8,128)}) fusion(bf16[16,16,256]{2,1,0:T(8,128)(2,1)S(1)} %copy-done.3, bf16[16,16,256]{2,1,0:T(8,128)(2,1)S(1)} %copy-done.1, f32[16,8,256]{2,1,0:T(8,128)S(1)} %get-tuple-element.194, f32[16,16,256]{2,1,0:T(8,128)S(1)} %get-tuple-element.170, f32[]{:T(128)} %bitcast.49, ...), kind=kLoop, calls=%fused_computation.188 | loop fusion | flops 3932160 | bytes 1179716 | tf_op jit(solution)/shard_map/convert_element_type | solution.py:175
  (130 shorter events, 30.5 us)
Async XLA Ops:
  7.2 47.8 %all-gather.3.cloned.1.call-start = ((), (), s32[]{:S(2)}) async-start(), calls=%async_computation | async-start | bytes 2228224 | tf_op jit(solution)/shard_map/all_gather | solution.py:142
  7.9 146.5 %all-gather.5.cloned.1.call-start = ((), (), s32[]{:S(2)}) async-start(), calls=%async_computation.1 | async-start | bytes 2228224 | tf_op jit(solution)/shard_map/all_gather | solution.py:142
  8.2 46.8 %copy-start.5 = (bf16[256,31]{0,1:T(8,128)(2,1)}, bf16[256,31]{0,1:T(8,128)(2,1)S(1)}, u32[]{:S(2)}) copy-start(bf16[256,31]{0,1:T(8,128)(2,1)S(1)} %get-tuple-element.235) | copy-start | bytes 47620
  67.1 17.3 %copy-start.8 = (pred[16]{0:T(512)(128)(4,1)S(1)}, pred[16]{0:T(512)(128)(4,1)}, u32[]{:S(2)}) copy-start(pred[16]{0:T(512)(128)(4,1)} %get-tuple-element.211) | copy-start | bytes 52
  67.1 17.3 %copy-start.10 = (f32[16]{0:T(128)S(1)}, f32[16]{0:T(128)}, u32[]{:S(2)}) copy-start(f32[16]{0:T(128)} %get-tuple-element.210) | copy-start | bytes 196
  68.2 34.5 %copy-start.7 = (f32[16]{0:T(128)S(1)}, f32[16]{0:T(128)}, u32[]{:S(2)}) copy-start(f32[16]{0:T(128)} %get-tuple-element.171) | copy-start | bytes 196
  68.2 8.0 %collective-permute-start = (f32[16,16,8]{2,1,0:T(8,128)S(1)}, f32[16,16,8]{2,1,0:T(8,128)S(1)}, u32[]{:S(2)}, u32[]{:S(2)}) collective-permute-start(f32[16,16,8]{2,1,0:T(8,128)S(1)} %get-tuple-element.203), channel_id=1, source_target_pairs={{0,1},{1,2},{2,3},{3,4},{4,5},{5,6},{6,7},{7,8},{8,9},{9,10},{10,1... | collective-permute-start | bytes 24584 | tf_op jit(solution)/shard_map/ppermute | solution.py:17
  74.1 9.7 %collective-permute-start.1 = (f32[16,16,8]{2,1,0:T(8,128)S(1)}, f32[16,16,8]{2,1,0:T(8,128)S(1)}, u32[]{:S(2)}, u32[]{:S(2)}) collective-permute-start(f32[16,16,8]{2,1,0:T(8,128)S(1)} %get-tuple-element.204), channel_id=1, source_target_pairs={{1,0},{2,1},{3,2},{4,3},{5,4},{6,5},{7,6},{8,7},{9,8},{10,9},{11,1... | collective-permute-start | bytes 24584 | tf_op jit(solution)/shard_map/ppermute | solution.py:17
  77.8 25.0 %copy-start.2 = (bf16[16,16,256]{2,1,0:T(8,128)(2,1)S(1)}, bf16[16,16,256]{2,1,0:T(8,128)(2,1)}, u32[]{:S(2)}) copy-start(bf16[16,16,256]{2,1,0:T(8,128)(2,1)} %param.13) | copy-start | bytes 393220
  77.9 25.0 %copy-start.4 = (bf16[16,16,256]{2,1,0:T(8,128)(2,1)S(1)}, bf16[16,16,256]{2,1,0:T(8,128)(2,1)}, u32[]{:S(2)}) copy-start(bf16[16,16,256]{2,1,0:T(8,128)(2,1)} %param.12) | copy-start | bytes 393220
  96.7 57.7 %copy-start.6 = (bf16[256,31]{0,1:T(8,128)(2,1)S(1)}, bf16[256,31]{0,1:T(8,128)(2,1)}, u32[]{:S(2)}) copy-start(bf16[256,31]{0,1:T(8,128)(2,1)} %copy-done.5) | copy-start | bytes 47620
  96.7 3.5 %collective-permute-start.2 = (bf16[16,8,256]{2,1,0:T(8,128)(2,1)S(1)}, bf16[16,8,256]{2,1,0:T(8,128)(2,1)S(1)}, u32[]{:S(2)}, u32[]{:S(2)}) collective-permute-start(bf16[16,8,256]{2,1,0:T(8,128)(2,1)S(1)} %get-tuple-element.207), channel_id=1, source_target_pairs={{0,32},{32,64},{64,96},{96,128},{128,160},{160,192},{192,224},{224... | collective-permute-start | bytes 196616 | tf_op jit(solution)/shard_map/ppermute | solution.py:27
  98.9 3.8 %collective-permute-start.3 = (bf16[16,8,256]{2,1,0:T(8,128)(2,1)S(1)}, bf16[16,8,256]{2,1,0:T(8,128)(2,1)S(1)}, u32[]{:S(2)}, u32[]{:S(2)}) collective-permute-start(bf16[16,8,256]{2,1,0:T(8,128)(2,1)S(1)} %get-tuple-element.208), channel_id=1, source_target_pairs={{32,0},{64,32},{96,64},{128,96},{160,128},{192,160},{224,192},{256... | collective-permute-start | bytes 196616 | tf_op jit(solution)/shard_map/ppermute | solution.py:29
  99.0 58.0 %copy-start.15 = (f32[16]{0:T(128)}, f32[16]{0:T(128)S(1)}, u32[]{:S(2)}) copy-start(f32[16]{0:T(128)S(1)} %add_convert_fusion.2) | copy-start | bytes 196
  158.4 8.2 %copy-start.14 = (f32[16]{0:T(128)S(1)}, f32[16]{0:T(128)}, u32[]{:S(2)}) copy-start(f32[16]{0:T(128)} %compare_select_fusion.2) | copy-start | bytes 196
  158.4 17.3 %copy-start.9 = (pred[16]{0:T(512)(128)(4,1)S(1)}, pred[16]{0:T(512)(128)(4,1)}, u32[]{:S(2)}) copy-start(pred[16]{0:T(512)(128)(4,1)} %get-tuple-element.175) | copy-start | bytes 52
  158.4 17.3 %copy-start.11 = (f32[16]{0:T(128)S(1)}, f32[16]{0:T(128)}, u32[]{:S(2)}) copy-start(f32[16]{0:T(128)} %get-tuple-element.209) | copy-start | bytes 196
  167.7 33.1 %copy-start.16 = (f32[16]{0:T(128)S(1)}, f32[16]{0:T(128)}, u32[]{:S(2)}) copy-start(f32[16]{0:T(128)} %copy-done.15) | copy-start | bytes 196
  167.8 7.1 %collective-permute-start.4 = (f32[16,16,8]{2,1,0:T(8,128)S(1)}, f32[16,16,8]{2,1,0:T(8,128)S(1)}, u32[]{:S(2)}, u32[]{:S(2)}) collective-permute-start(f32[16,16,8]{2,1,0:T(8,128)S(1)} %get-tuple-element.197), channel_id=1, source_target_pairs={{0,1},{1,2},{2,3},{3,4},{4,5},{5,6},{6,7},{7,8},{8,9},{9,10},{10,1... | collective-permute-start | bytes 24584 | tf_op jit(solution)/shard_map/ppermute | solution.py:17
  172.2 9.7 %collective-permute-start.5 = (f32[16,16,8]{2,1,0:T(8,128)S(1)}, f32[16,16,8]{2,1,0:T(8,128)S(1)}, u32[]{:S(2)}, u32[]{:S(2)}) collective-permute-start(f32[16,16,8]{2,1,0:T(8,128)S(1)} %get-tuple-element.198), channel_id=1, source_target_pairs={{1,0},{2,1},{3,2},{4,3},{5,4},{6,5},{7,6},{8,7},{9,8},{10,9},{11,1... | collective-permute-start | bytes 24584 | tf_op jit(solution)/shard_map/ppermute | solution.py:17
  175.8 25.1 %copy-start.1 = (bf16[16,16,256]{2,1,0:T(8,128)(2,1)S(1)}, bf16[16,16,256]{2,1,0:T(8,128)(2,1)}, u32[]{:S(2)}) copy-start(bf16[16,16,256]{2,1,0:T(8,128)(2,1)} %copy-done) | copy-start | bytes 393220
  175.8 25.1 %copy-start.3 = (bf16[16,16,256]{2,1,0:T(8,128)(2,1)S(1)}, bf16[16,16,256]{2,1,0:T(8,128)(2,1)}, u32[]{:S(2)}) copy-start(bf16[16,16,256]{2,1,0:T(8,128)(2,1)} %param.13) | copy-start | bytes 393220
  194.9 3.5 %collective-permute-start.6 = (bf16[16,8,256]{2,1,0:T(8,128)(2,1)S(1)}, bf16[16,8,256]{2,1,0:T(8,128)(2,1)S(1)}, u32[]{:S(2)}, u32[]{:S(2)}) collective-permute-start(bf16[16,8,256]{2,1,0:T(8,128)(2,1)S(1)} %get-tuple-element.205), channel_id=1, source_target_pairs={{0,32},{32,64},{64,96},{96,128},{128,160},{160,192},{192,224},{224... | collective-permute-start | bytes 196616 | tf_op jit(solution)/shard_map/ppermute | solution.py:27
  197.0 3.8 %collective-permute-start.7 = (bf16[16,8,256]{2,1,0:T(8,128)(2,1)S(1)}, bf16[16,8,256]{2,1,0:T(8,128)(2,1)S(1)}, u32[]{:S(2)}, u32[]{:S(2)}) collective-permute-start(bf16[16,8,256]{2,1,0:T(8,128)(2,1)S(1)} %get-tuple-element.206), channel_id=1, source_target_pairs={{32,0},{64,32},{96,64},{128,96},{160,128},{192,160},{224,192},{256... | collective-permute-start | bytes 196616 | tf_op jit(solution)/shard_map/ppermute | solution.py:29
  (5 other events, 21.7 us)
Sparse Core Ops, SparseCore 0:
  10.2 44.7 all-gather.2
  115.7 38.6 all-gather.4
where the time goes:
time: 221 us; the launch traced here: 220 us
  waiting for transfers between devices  98.1 us (44%)
  other arithmetic  63.5 us (29%)
  starting transfers between devices  17.3 us (8%)
  matrix products  15.4 us (7%)
  between operations  14.5 us (7%)
  local copies, waits for them, and re-layouts  10.8 us (5%)
    all_gather x2, waiting for transfers between devices, body(): whole_tiles = lax.all_gather(work_tiles, 'segment', axis=1, tiled=True)  77.3 us
    convert_element_type x2, other arithmetic, body(): horiz_blur.astype(jnp.bfloat16)  24.4 us
    convert_element_type x2, other arithmetic, body(): mask_now = (mask_now.astype(jnp.float32) + STEP_GAIN * (tile_target_image...  23.5 us
    ppermute x4, starting transfers between devices, passed_along(): return lax.ppermute(block, axis, route)  13 us
    ppermute x4, waiting for transfers between devices, passed_along(): return lax.ppermute(block, axis, route)  12.7 us
    dot_general x4, matrix products, one_block(): jnp.einsum('nkrb,by->nkry', field_a, inverse_cols, preferred_element_type...  10.4 us
    dot_general x2, matrix products, spectrum_part(): jnp.einsum('ra,nrb->nab', rows_table, y_part, preferred_element_type=jnp....  5.01 us
    ppermute x2, waiting for transfers between devices, with_halo(): lax.ppermute(head, axis, [((i + 1) % count, i) for i in range(count)])  4.87 us
  transfers between devices with their start and end apart: 10, of which 9 were waited for; matrix products, arithmetic and copies ran while one was open for 6% of the time, Pallas kernels for 0%

commit v1 on v0

--- a/solution.py
+++ b/solution.py
@@ -139,7 +139,10 @@
     resist = jnp.zeros((slot_count, row_count, tile_edge), jnp.float32)
     for sweep in range(ITERS):
         work_tiles = mask_now
-        whole_tiles = lax.all_gather(work_tiles, "segment", axis=1, tiled=True)
+        whole_tiles = jnp.concatenate(
+            lax.all_to_all(jnp.stack([work_tiles] * lax.axis_size("segment")), "segment", 0, 0),
+            axis=1,
+        )
         spectrum = spectrum_part(whole_tiles, forward_rows, forward_cols, freq_count)
         intensity = intensity_rows(spectrum, spectra, rows_inverse, inverse_cols, tile_edge)
         intensity = intensity * weight[:, None, None]

time: 221 us -> 233 us (1.054)
  the two profiles are of different devices: /device:TPU:199 before, /device:TPU:255 now
where the time goes in v1:
time: 233 us; the launch traced here: 231 us
  other arithmetic  63.6 us (27%)
  waiting for transfers between devices  59.7 us (26%)
  blocking collectives  51.5 us (22%)
  starting transfers between devices  28.1 us (12%)
  matrix products  13.8 us (6%)
  local copies, waits for them, and re-layouts  13.4 us (6%)
    all_to_all x1, blocking collectives, body(): lax.all_to_all(jnp.stack([work_tiles] * lax.axis_size('segment')), 'segme...  51.5 us
    all_to_all x1, waiting for transfers between devices, body(): lax.all_to_all(jnp.stack([work_tiles] * lax.axis_size('segment')), 'segme...  39.6 us
    convert_element_type x2, other arithmetic, body(): horiz_blur.astype(jnp.bfloat16)  24.4 us
    convert_element_type x2, other arithmetic, body(): mask_now = (mask_now.astype(jnp.float32) + STEP_GAIN * (tile_target_image...  23.5 us
    ppermute x4, starting transfers between devices, passed_along(): return lax.ppermute(block, axis, route)  12.3 us
    dot_general x4, matrix products, one_block(): jnp.einsum('nkrb,by->nkry', field_a, inverse_cols, preferred_element_type...  10.4 us
    ppermute x4, waiting for transfers between devices, passed_along(): return lax.ppermute(block, axis, route)  10.3 us
    ppermute x2, starting transfers between devices, with_halo(): lax.ppermute(tail, axis, [(i, (i + 1) % count) for i in range(count)])  8.44 us
  transfers between devices with their start and end apart: 9, of which 8 were waited for; matrix products, arithmetic and copies ran while one was open for 5% of the time, Pallas kernels for 0%

profile of v1, /device:TPU:255, one launch (start us, length us, event | category | flops | bytes accessed | tf_op | source)
XLA Modules:
  0.0 231.4 jit_solution(15164093756200010765)
XLA Ops:
  0.6 2.5 %stack.16 = bf16[16,16,16,256]{3,2,1,0:T(8,128)(2,1)} broadcast(bf16[16,16,256]{2,1,0:T(8,128)(2,1)} %param.12), dimensions={1,2,3} | broadcast | bytes 2228224 | tf_op jit(solution)/shard_map/stack | solution.py:143
  3.1 7.3 %all-to-all-start = ((bf16[16,16,16,256]{3,2,1,0:T(8,128)(2,1)}), bf16[16,16,16,256]{3,2,1,0:T(8,128)(2,1)S(1)}, u32[]{:S(2)}, u32[]{:S(2)}) async-start(bf16[16,16,16,256]{3,2,1,0:T(8,128)(2,1)} %stack.16), calls=%async_computation | async-start | bytes 4194304 | tf_op jit(solution)/shard_map/all_to_all | solution.py:143
  17.9 39.6 %all-to-all-done = bf16[16,16,16,256]{3,2,1,0:T(8,128)(2,1)S(1)} async-done(((bf16[16,16,16,256]{3,2,1,0:T(8,128)(2,1)}), bf16[16,16,16,256]{3,2,1,0:T(8,128)(2,1)S(1)}, u32[]{:S(2)}, u32[]{:S(2)}) %all-to-all-start) | async-done | bytes 2097184 | tf_op jit(solution)/shard_map/all_to_all | solution.py:143
  59.1 2.5 %fusion.62 = f32[16,62,62]{1,2,0:T(8,128)S(1)} fusion(bf16[16,256,256]{2,1,0:T(8,128)(2,1)} %bitcast.159, bf16[256,31]{0,1:T(8,128)(2,1)S(1)} %get-tuple-element.236, bf16[256,31]{0,1:T(8,128)(2,1)S(1)} %get-tuple-element.234, bf16[256,31]{0,1:T(8,128)(2,1)S(1)} %get-tuple-element.235), kind=kOutput, calls=%fused_computation.62 | convolution fusion | flops 161894400 | bytes 2390784 | tf_op jit(solution)/shard_map/ra,nrb->nab/dot_general | solution.py:73
  63.0 8.2 %while.20 = (s32[]{:T(128)}, f32[2,8,16,256]{3,2,1,0:T(8,128)}, f32[12,1,31,31]{3,2,0,1:T(8,128)S(1)}, f32[2,8,2,31,31]{4,1,3,2,0:T(8,128)S(1)}, f32[12,1,31,31]...) while((s32[]{:T(128)}, f32[2,8,16,256]{3,2,1,0:T(8,128)}, ...), condition=%wide.region_3.4_spmd, body=%wide.region_1.3_spmd.sunk | while | flops 115241184 | bytes 2505049 | solution.py:113
  63.8 2.6 %multiply_reduce_fusion.4 = f32[8,16,512]{2,1,0:T(8,128)S(1)} fusion(bf16[8,12,31,31]{3,2,1,0:T(8,128)(2,1)S(1)} %get-tuple-element.326, bf16[8,12,31,31]{3,2,1,0:T(8,128)(2,1)S(1)} %fusion.329, bf16[8,12,31,31]{3,2,1,0:T(8,128)(2,1)S(1)} %get-tuple-element.327, bf16[62,512]{1,0:T(8,128)(2,1)} %get-tuple-element.361, ...), kind=kOutput, calls=%fused_computation.4.clone.1 | convolution fusion | flops 113976320 | bytes 881152 | tf_op jit(solution)/shard_map/while/body/eval_jaxpr/nkrb,by->nkry/dot_general | solution.py:104
  67.9 2.6 %multiply_reduce_fusion.4 = f32[8,16,512]{2,1,0:T(8,128)S(1)} fusion(bf16[8,12,31,31]{3,2,1,0:T(8,128)(2,1)S(1)} %get-tuple-element.326, bf16[8,12,31,31]{3,2,1,0:T(8,128)(2,1)S(1)} %fusion.329, bf16[8,12,31,31]{3,2,1,0:T(8,128)(2,1)S(1)} %get-tuple-element.327, bf16[62,512]{1,0:T(8,128)(2,1)} %get-tuple-element.361, ...), kind=kOutput, calls=%fused_computation.4.clone.1 | convolution fusion | flops 113976320 | bytes 881152 | tf_op jit(solution)/shard_map/while/body/eval_jaxpr/nkrb,by->nkry/dot_general | solution.py:104
  72.4 5.1 %collective-permute-start = (f32[16,16,8]{2,1,0:T(8,128)S(1)}, f32[16,16,8]{2,1,0:T(8,128)S(1)}, u32[]{:S(2)}, u32[]{:S(2)}) collective-permute-start(f32[16,16,8]{2,1,0:T(8,128)S(1)} %get-tuple-element.203), channel_id=1, source_target_pairs={{0,1},{1,2},{2,3},{3,4},{4,5},{5,6},{6,7},{7,8},{8,9},{9,10},{10,1... | collective-permute-start | bytes 24584 | tf_op jit(solution)/shard_map/ppermute | solution.py:17
  82.5 5.4 %collective-permute-done.1 = f32[16,16,8]{2,1,0:T(8,128)S(1)} collective-permute-done((f32[16,16,8]{2,1,0:T(8,128)S(1)}, f32[16,16,8]{2,1,0:T(8,128)S(1)}, u32[]{:S(2)}, u32[]{:S(2)}) %collective-permute-start.1) | collective-permute-done | bytes 8224 | tf_op jit(solution)/shard_map/ppermute | solution.py:17
  88.6 12.2 %fusion.306 = (bf16[16,16,256]{2,1,0:T(8,128)(2,1)S(1)}, f32[16,16,256]{2,1,0:T(8,128)S(1)}) fusion(f32[16,16,8]{2,1,0:T(8,128)S(1)} %select_multiply_fusion.1, f32[16,16,256]{2,1,0:T(8,128)S(1)} %bitcast_multiply_fusion.1, f32[]{:T(128)} %bitcast.51, f32[]{:T(128)} %bitcast.50, f32[]{:T(128)} %bitcast.49, f32[]{:T(128)} %bitcast.48, f32[]{:T(128)} %bitcast.47, ...), kind=kLoop, calls=%fused_computation.472 | loop fusion | flops 3276800 | bytes 671812 | tf_op jit(solution)/shard_map/convert_element_type | solution.py:159
  100.8 3.9 %collective-permute-start.2 = (bf16[16,8,256]{2,1,0:T(8,128)(2,1)S(1)}, bf16[16,8,256]{2,1,0:T(8,128)(2,1)S(1)}, u32[]{:S(2)}, u32[]{:S(2)}) collective-permute-start(bf16[16,8,256]{2,1,0:T(8,128)(2,1)S(1)} %get-tuple-element.207), channel_id=1, source_target_pairs={{0,32},{32,64},{64,96},{96,128},{128,160},{160,192},{192,224},{224... | collective-permute-start | bytes 196616 | tf_op jit(solution)/shard_map/ppermute | solution.py:27
  106.1 3.6 %collective-permute-done.3 = bf16[16,8,256]{2,1,0:T(8,128)(2,1)S(1)} collective-permute-done((bf16[16,8,256]{2,1,0:T(8,128)(2,1)S(1)}, bf16[16,8,256]{2,1,0:T(8,128)(2,1)S(1)}, u32[]{:S(2)}, u32[]{:S(2)}) %collective-permute-start.3) | collective-permute-done | bytes 65568 | tf_op jit(solution)/shard_map/ppermute | solution.py:29
  109.8 11.4 %fusion.67 = bf16[16,16,256]{2,1,0:T(8,128)(2,1)S(1)} fusion(bf16[16,16,256]{2,1,0:T(8,128)(2,1)S(1)} %copy-done.3, f32[16,16,256]{2,1,0:T(8,128)S(1)} %get-tuple-element.174, f32[16,8,256]{2,1,0:T(8,128)S(1)} %get-tuple-element.200, f32[16,8,256]{2,1,0:T(8,128)S(1)} %get-tuple-element.199, bf16[16,16,256]{2,1,0:T(8,128)(2,1)S(1)} %copy-done.2, ...), kind=kLoop, calls=%fused_computation.183 | loop fusion | flops 3932160 | bytes 917572 | tf_op jit(solution)/shard_map/convert_element_type | solution.py:178
  121.4 51.5 %all_to_all.10 = bf16[16,16,16,256]{3,2,1,0:T(8,128)(2,1)S(1)} all-to-all(bf16[16,16,16,256]{3,2,1,0:T(8,128)(2,1)S(1)} %stack.20), channel_id=1, replica_groups=mesh['segment'=16,'tile'=32] {'segment'}, dimensions={0} | all-to-all | bytes 4194304 | tf_op jit(solution)/shard_map/all_to_all | solution.py:143
  176.0 8.2 %while.21 = (s32[]{:T(128)}, f32[2,8,16,256]{3,2,1,0:T(8,128)}, f32[12,1,31,31]{3,2,0,1:T(8,128)S(1)}, f32[2,8,2,31,31]{4,1,3,2,0:T(8,128)S(1)}, f32[12,1,31,31]...) while((s32[]{:T(128)}, f32[2,8,16,256]{3,2,1,0:T(8,128)}, ...), condition=%wide.region_6.8_spmd, body=%wide.region_4.7_spmd.sunk | while | flops 115241184 | bytes 2505049 | solution.py:113
  176.9 2.6 %multiply_reduce_fusion.5 = f32[8,16,512]{2,1,0:T(8,128)S(1)} fusion(bf16[8,12,31,31]{3,2,1,0:T(8,128)(2,1)S(1)} %get-tuple-element.337, bf16[8,12,31,31]{3,2,1,0:T(8,128)(2,1)S(1)} %fusion.334, bf16[8,12,31,31]{3,2,1,0:T(8,128)(2,1)S(1)} %get-tuple-element.338, bf16[62,512]{1,0:T(8,128)(2,1)} %get-tuple-element.385, ...), kind=kOutput, calls=%fused_computation.31.clone.1 | convolution fusion | flops 113976320 | bytes 881152 | tf_op jit(solution)/shard_map/while/body/eval_jaxpr/nkrb,by->nkry/dot_general | solution.py:104
  181.0 2.6 %multiply_reduce_fusion.5 = f32[8,16,512]{2,1,0:T(8,128)S(1)} fusion(bf16[8,12,31,31]{3,2,1,0:T(8,128)(2,1)S(1)} %get-tuple-element.337, bf16[8,12,31,31]{3,2,1,0:T(8,128)(2,1)S(1)} %fusion.334, bf16[8,12,31,31]{3,2,1,0:T(8,128)(2,1)S(1)} %get-tuple-element.338, bf16[62,512]{1,0:T(8,128)(2,1)} %get-tuple-element.385, ...), kind=kOutput, calls=%fused_computation.31.clone.1 | convolution fusion | flops 113976320 | bytes 881152 | tf_op jit(solution)/shard_map/while/body/eval_jaxpr/nkrb,by->nkry/dot_general | solution.py:104
  185.4 1.9 collective-permute-start.4
  187.3 3.4 %collective-permute-start.5 = (f32[16,16,8]{2,1,0:T(8,128)S(1)}, f32[16,16,8]{2,1,0:T(8,128)S(1)}, u32[]{:S(2)}, u32[]{:S(2)}) collective-permute-start(f32[16,16,8]{2,1,0:T(8,128)S(1)} %get-tuple-element.198), channel_id=1, source_target_pairs={{1,0},{2,1},{3,2},{4,3},{5,4},{6,5},{7,6},{8,7},{9,8},{10,9},{11,1... | collective-permute-start | bytes 24584 | tf_op jit(solution)/shard_map/ppermute | solution.py:17
  192.5 4.2 %collective-permute-done.5 = f32[16,16,8]{2,1,0:T(8,128)S(1)} collective-permute-done((f32[16,16,8]{2,1,0:T(8,128)S(1)}, f32[16,16,8]{2,1,0:T(8,128)S(1)}, u32[]{:S(2)}, u32[]{:S(2)}) %collective-permute-start.5) | collective-permute-done | bytes 8224 | tf_op jit(solution)/shard_map/ppermute | solution.py:17
  197.5 12.2 %fusion.303 = (bf16[16,16,256]{2,1,0:T(8,128)(2,1)S(1)}, f32[16,16,256]{2,1,0:T(8,128)S(1)}) fusion(f32[16,16,8]{2,1,0:T(8,128)S(1)} %select_multiply_fusion, f32[16,16,256]{2,1,0:T(8,128)S(1)} %bitcast_multiply_fusion, f32[]{:T(128)} %bitcast.51, f32[]{:T(128)} %bitcast.50, f32[]{:T(128)} %bitcast.49, f32[]{:T(128)} %bitcast.48, f32[]{:T(128)} %bitcast.47, ...), kind=kLoop, calls=%fused_computation.470 | loop fusion | flops 3276800 | bytes 671812 | tf_op jit(solution)/shard_map/convert_element_type | solution.py:159
  209.7 4.5 %collective-permute-start.6 = (bf16[16,8,256]{2,1,0:T(8,128)(2,1)S(1)}, bf16[16,8,256]{2,1,0:T(8,128)(2,1)S(1)}, u32[]{:S(2)}, u32[]{:S(2)}) collective-permute-start(bf16[16,8,256]{2,1,0:T(8,128)(2,1)S(1)} %get-tuple-element.205), channel_id=1, source_target_pairs={{0,32},{32,64},{64,96},{96,128},{128,160},{160,192},{192,224},{224... | collective-permute-start | bytes 196616 | tf_op jit(solution)/shard_map/ppermute | solution.py:27
  215.6 3.6 %collective-permute-done.7 = bf16[16,8,256]{2,1,0:T(8,128)(2,1)S(1)} collective-permute-done((bf16[16,8,256]{2,1,0:T(8,128)(2,1)S(1)}, bf16[16,8,256]{2,1,0:T(8,128)(2,1)S(1)}, u32[]{:S(2)}, u32[]{:S(2)}) %collective-permute-start.7) | collective-permute-done | bytes 65568 | tf_op jit(solution)/shard_map/ppermute | solution.py:29
  219.3 12.1 %fusion.70 = (bf16[16,16,256]{2,1,0:T(8,128)(2,1)}, f32[16,16,256]{2,1,0:T(8,128)}) fusion(bf16[16,16,256]{2,1,0:T(8,128)(2,1)S(1)} %copy-done.4, bf16[16,16,256]{2,1,0:T(8,128)(2,1)S(1)} %copy-done.1, f32[16,8,256]{2,1,0:T(8,128)S(1)} %get-tuple-element.194, f32[16,16,256]{2,1,0:T(8,128)S(1)} %get-tuple-element.170, f32[]{:T(128)} %bitcast.51, ...), kind=kLoop, calls=%fused_computation.186 | loop fusion | flops 3932160 | bytes 1179716 | tf_op jit(solution)/shard_map/convert_element_type | solution.py:178
  (140 shorter events, 32.8 us)
Async XLA Ops:
  3.1 54.4 %all-to-all-start = ((bf16[16,16,16,256]{3,2,1,0:T(8,128)(2,1)}), bf16[16,16,16,256]{3,2,1,0:T(8,128)(2,1)S(1)}, u32[]{:S(2)}, u32[]{:S(2)}) async-start(bf16[16,16,16,256]{3,2,1,0:T(8,128)(2,1)} %stack.16), calls=%async_computation | async-start | bytes 4194304 | tf_op jit(solution)/shard_map/all_to_all | solution.py:143
  10.7 48.4 %copy-start.6 = (bf16[256,31]{0,1:T(8,128)(2,1)}, bf16[256,31]{0,1:T(8,128)(2,1)S(1)}, u32[]{:S(2)}) copy-start(bf16[256,31]{0,1:T(8,128)(2,1)S(1)} %get-tuple-element.235) | copy-start | bytes 47620
  71.2 17.3 %copy-start.11 = (pred[16]{0:T(512)(128)(4,1)S(1)}, pred[16]{0:T(512)(128)(4,1)}, u32[]{:S(2)}) copy-start(pred[16]{0:T(512)(128)(4,1)} %get-tuple-element.211) | copy-start | bytes 52
  71.2 17.3 %copy-start.14 = (f32[16]{0:T(128)S(1)}, f32[16]{0:T(128)}, u32[]{:S(2)}) copy-start(f32[16]{0:T(128)} %get-tuple-element.210) | copy-start | bytes 196
  72.3 37.4 %copy-start.9 = (f32[16]{0:T(128)S(1)}, f32[16]{0:T(128)}, u32[]{:S(2)}) copy-start(f32[16]{0:T(128)} %get-tuple-element.171) | copy-start | bytes 196
  72.4 8.5 %collective-permute-start = (f32[16,16,8]{2,1,0:T(8,128)S(1)}, f32[16,16,8]{2,1,0:T(8,128)S(1)}, u32[]{:S(2)}, u32[]{:S(2)}) collective-permute-start(f32[16,16,8]{2,1,0:T(8,128)S(1)} %get-tuple-element.203), channel_id=1, source_target_pairs={{0,1},{1,2},{2,3},{3,4},{4,5},{5,6},{6,7},{7,8},{8,9},{9,10},{10,1... | collective-permute-start | bytes 24584 | tf_op jit(solution)/shard_map/ppermute | solution.py:17
  78.2 31.7 %copy-start.8 = (s32[1024]{0:T(1024)}, s32[1024]{0:T(1024)S(1)}, u32[]{:S(2)}) copy-start(s32[1024]{0:T(1024)S(1)} %pad_clamp_fusion) | copy-start | bytes 12292
  78.9 9.0 %collective-permute-start.1 = (f32[16,16,8]{2,1,0:T(8,128)S(1)}, f32[16,16,8]{2,1,0:T(8,128)S(1)}, u32[]{:S(2)}, u32[]{:S(2)}) collective-permute-start(f32[16,16,8]{2,1,0:T(8,128)S(1)} %get-tuple-element.204), channel_id=1, source_target_pairs={{1,0},{2,1},{3,2},{4,3},{5,4},{6,5},{7,6},{8,7},{9,8},{10,9},{11,1... | collective-permute-start | bytes 24584 | tf_op jit(solution)/shard_map/ppermute | solution.py:17
  82.5 27.3 %copy-start.2 = (bf16[16,16,256]{2,1,0:T(8,128)(2,1)S(1)}, bf16[16,16,256]{2,1,0:T(8,128)(2,1)}, u32[]{:S(2)}) copy-start(bf16[16,16,256]{2,1,0:T(8,128)(2,1)} %param.12) | copy-start | bytes 393220
  82.5 27.3 %copy-start.3 = (bf16[16,16,256]{2,1,0:T(8,128)(2,1)S(1)}, bf16[16,16,256]{2,1,0:T(8,128)(2,1)}, u32[]{:S(2)}) copy-start(bf16[16,16,256]{2,1,0:T(8,128)(2,1)} %param.13) | copy-start | bytes 393220
  100.8 5.3 %collective-permute-start.2 = (bf16[16,8,256]{2,1,0:T(8,128)(2,1)S(1)}, bf16[16,8,256]{2,1,0:T(8,128)(2,1)S(1)}, u32[]{:S(2)}, u32[]{:S(2)}) collective-permute-start(bf16[16,8,256]{2,1,0:T(8,128)(2,1)S(1)} %get-tuple-element.207), channel_id=1, source_target_pairs={{0,32},{32,64},{64,96},{96,128},{128,160},{160,192},{192,224},{224... | collective-permute-start | bytes 196616 | tf_op jit(solution)/shard_map/ppermute | solution.py:27
  104.8 4.9 %collective-permute-start.3 = (bf16[16,8,256]{2,1,0:T(8,128)(2,1)S(1)}, bf16[16,8,256]{2,1,0:T(8,128)(2,1)S(1)}, u32[]{:S(2)}, u32[]{:S(2)}) collective-permute-start(bf16[16,8,256]{2,1,0:T(8,128)(2,1)S(1)} %get-tuple-element.208), channel_id=1, source_target_pairs={{32,0},{64,32},{96,64},{128,96},{160,128},{192,160},{224,192},{256... | collective-permute-start | bytes 196616 | tf_op jit(solution)/shard_map/ppermute | solution.py:29
  104.9 16.6 %copy-start.20 = (f32[16]{0:T(128)}, f32[16]{0:T(128)S(1)}, u32[]{:S(2)}) copy-start(f32[16]{0:T(128)S(1)} %add_convert_fusion.2) | copy-start | bytes 196
  121.2 51.8 %copy-start = (bf16[16,16,256]{2,1,0:T(8,128)(2,1)}, bf16[16,16,256]{2,1,0:T(8,128)(2,1)S(1)}, u32[]{:S(2)}) copy-start(bf16[16,16,256]{2,1,0:T(8,128)(2,1)S(1)} %fusion.67) | copy-start | bytes 393220
  176.0 16.2 %copy-start.13 = (pred[16]{0:T(512)(128)(4,1)S(1)}, pred[16]{0:T(512)(128)(4,1)}, u32[]{:S(2)}) copy-start(pred[16]{0:T(512)(128)(4,1)} %get-tuple-element.175) | copy-start | bytes 52
  176.0 16.2 %copy-start.16 = (f32[16]{0:T(128)S(1)}, f32[16]{0:T(128)}, u32[]{:S(2)}) copy-start(f32[16]{0:T(128)} %get-tuple-element.209) | copy-start | bytes 196
  185.4 33.8 %copy-start.10 = (f32[16]{0:T(128)S(1)}, f32[16]{0:T(128)}, u32[]{:S(2)}) copy-start(f32[16]{0:T(128)} %get-tuple-element.171) | copy-start | bytes 196
  185.4 33.8 %copy-start.21 = (f32[16]{0:T(128)S(1)}, f32[16]{0:T(128)}, u32[]{:S(2)}) copy-start(f32[16]{0:T(128)} %copy-done.20) | copy-start | bytes 196
  185.4 6.0 %collective-permute-start.4 = (f32[16,16,8]{2,1,0:T(8,128)S(1)}, f32[16,16,8]{2,1,0:T(8,128)S(1)}, u32[]{:S(2)}, u32[]{:S(2)}) collective-permute-start(f32[16,16,8]{2,1,0:T(8,128)S(1)} %get-tuple-element.197), channel_id=1, source_target_pairs={{0,1},{1,2},{2,3},{3,4},{4,5},{5,6},{6,7},{7,8},{8,9},{9,10},{10,1... | collective-permute-start | bytes 24584 | tf_op jit(solution)/shard_map/ppermute | solution.py:17
  187.3 9.3 %collective-permute-start.5 = (f32[16,16,8]{2,1,0:T(8,128)S(1)}, f32[16,16,8]{2,1,0:T(8,128)S(1)}, u32[]{:S(2)}, u32[]{:S(2)}) collective-permute-start(f32[16,16,8]{2,1,0:T(8,128)S(1)} %get-tuple-element.198), channel_id=1, source_target_pairs={{1,0},{2,1},{3,2},{4,3},{5,4},{6,5},{7,6},{8,7},{9,8},{10,9},{11,1... | collective-permute-start | bytes 24584 | tf_op jit(solution)/shard_map/ppermute | solution.py:17
  192.4 27.0 %copy-start.1 = (bf16[16,16,256]{2,1,0:T(8,128)(2,1)S(1)}, bf16[16,16,256]{2,1,0:T(8,128)(2,1)}, u32[]{:S(2)}) copy-start(bf16[16,16,256]{2,1,0:T(8,128)(2,1)} %copy-done) | copy-start | bytes 393220
  192.4 26.9 %copy-start.4 = (bf16[16,16,256]{2,1,0:T(8,128)(2,1)S(1)}, bf16[16,16,256]{2,1,0:T(8,128)(2,1)}, u32[]{:S(2)}) copy-start(bf16[16,16,256]{2,1,0:T(8,128)(2,1)} %param.13) | copy-start | bytes 393220
  209.7 5.8 %collective-permute-start.6 = (bf16[16,8,256]{2,1,0:T(8,128)(2,1)S(1)}, bf16[16,8,256]{2,1,0:T(8,128)(2,1)S(1)}, u32[]{:S(2)}, u32[]{:S(2)}) collective-permute-start(bf16[16,8,256]{2,1,0:T(8,128)(2,1)S(1)} %get-tuple-element.205), channel_id=1, source_target_pairs={{0,32},{32,64},{64,96},{96,128},{128,160},{160,192},{192,224},{224... | collective-permute-start | bytes 196616 | tf_op jit(solution)/shard_map/ppermute | solution.py:27
  214.2 4.9 %collective-permute-start.7 = (bf16[16,8,256]{2,1,0:T(8,128)(2,1)S(1)}, bf16[16,8,256]{2,1,0:T(8,128)(2,1)S(1)}, u32[]{:S(2)}, u32[]{:S(2)}) collective-permute-start(bf16[16,8,256]{2,1,0:T(8,128)(2,1)S(1)} %get-tuple-element.206), channel_id=1, source_target_pairs={{32,0},{64,32},{96,64},{128,96},{160,128},{192,160},{224,192},{256... | collective-permute-start | bytes 196616 | tf_op jit(solution)/shard_map/ppermute | solution.py:29
  (9 other events, 59.0 us)
